TPU v7x, 256 devices: a whole 4x4x8 slice. The times are simulated.
256 devices in a mesh: dp: 32 (over z, x_hi, core), fsdp: 8 (over x_lo, y).
Axes of the slice: x: 4 (x_hi: 2, x_lo: 2; x = x_hi * 2 + x_lo), y: 4, z: 8, core: 2. Of those that a mesh axis runs over, the one named last changes fastest.
Arguments:
- attn: bfloat16 [147456, 1536], P(('dp', 'fsdp')), may hold values from -6 to 6
- cotangent: bfloat16 [147456, 3072], P(('dp', 'fsdp')), may hold values from -24 to 24
- weight: bfloat16 [1536, 3072], P('fsdp'), may hold values from -0.15625 to 0.15625
- projector: bfloat16 [1536, 256], replicated, may hold values from -0.15625 to 0.15625
- moment_one: float32 [3072, 256], P(('dp', 'fsdp')), may hold values from -256 to 256
- moment_two: float32 [3072, 256], P(('dp', 'fsdp')), may hold values from 30 to 3000
- step_count: int32 [1], replicated, may hold values from 1 to 10
Outputs:
- grad_input: bfloat16 [147456, 1536], P(('dp', 'fsdp'))
- weight_step: float32 [1536, 3072], P('fsdp')
- first_moment: float32 [3072, 256], P(('dp', 'fsdp'))
- second_moment: float32 [3072, 256], P(('dp', 'fsdp'))
All inputs are finite; a program needn't handle non-finite values.
Results may differ from a plain program's by a relative error of at most 0.015.
Values may be sent and summed in bfloat16 or wider, within the bound.
A program may use at most 128 MiB of HBM per device.

v0:
```python
import jax
import jax.numpy as jnp
from jax import lax
from jax.sharding import PartitionSpec as P


def on_device(attn, cotangent, weight, projector, moment_one, moment_two, step_count):
    shard_rows = weight.shape[0]
    reduced = jnp.dot(attn, projector, preferred_element_type=jnp.float32).astype(jnp.bfloat16)
    grad_input = lax.dot_general(
        cotangent,
        lax.all_gather(weight, "fsdp", axis=0, tiled=True),
        (((1,), (1,)), ((), ())),
        preferred_element_type=jnp.float32,
    ).astype(jnp.bfloat16)
    projected = lax.psum_scatter(
        lax.dot_general(
            cotangent, reduced, (((0,), (0,)), ((), ())), preferred_element_type=jnp.float32
        ),
        ("dp", "fsdp"),
        scatter_dimension=0,
        tiled=True,
    )
    first_moment = 0.9 * moment_one + 0.1 * projected
    second_moment = 0.999 * moment_two + 0.001 * projected * projected
    steps = step_count[0].astype(jnp.float32)
    first_hat = first_moment / (1.0 - jnp.power(jnp.float32(0.9), steps))
    second_hat = second_moment / (1.0 - jnp.power(jnp.float32(0.999), steps))
    low_step = (first_hat / (jnp.sqrt(second_hat) + 1e-08)).astype(jnp.bfloat16)
    my_projector = lax.dynamic_slice_in_dim(
        projector, lax.axis_index("fsdp") * shard_rows, shard_rows, 0
    )
    weight_step = 0.25 * lax.dot_general(
        my_projector,
        lax.all_gather(low_step, ("dp", "fsdp"), axis=0, tiled=True),
        (((1,), (1,)), ((), ())),
        preferred_element_type=jnp.float32,
    )
    return (grad_input, weight_step, first_moment, second_moment)


def solution(mesh):
    placed = (
        P(("dp", "fsdp"), None),
        P(("dp", "fsdp"), None),
        P("fsdp", None),
        P(),
        P(("dp", "fsdp"), None),
        P(("dp", "fsdp"), None),
        P(),
    )
    return jax.shard_map(
        on_device,
        mesh=mesh,
        in_specs=placed,
        out_specs=(
            P(("dp", "fsdp"), None),
            P("fsdp", None),
            P(("dp", "fsdp"), None),
            P(("dp", "fsdp"), None),
        ),
        check_vma=False,
    )
```

profile of v0, /device:TPU:1, one launch (start us, length us, event | category | flops | bytes accessed | tf_op | source)
XLA Modules:
  0.0 1102.5 jit_solution(9740746356282910533)
XLA Ops:
  7.2 0.0 copy-start
  7.2 0.0 all-reduce.3.cloned.1.call-start
  7.2 1.9 copy-done
  9.2 6.2 convolution_bitcast_fusion
  15.4 0.0 all-reduce.3.cloned.1.call-update
  15.4 0.0 all-gather.6.cloned.1.call-start
  16.2 266.0 %all-reduce.3.cloned.1.call-done = f32[3072,256]{0,1:T(8,128)} async-done(((f32[3072,256]{0,1:T(8,128)}), f32[3072,256]{0,1:T(8,128)}) %all-reduce.3.cloned.1.call-update) | async-done | bytes 3145744
  282.2 1.7 constant_dynamic-slice_fusion
  283.9 1.0 copy.31
  284.9 1.4 fusion.2
  286.3 0.0 all-gather.6.cloned.1.call-update
  286.3 0.0 all-gather.4.cloned.1.call-start
  286.3 0.7 all-gather.4.cloned.1.call-update
  287.0 694.5 %all-gather.6.cloned.1.call-done = bf16[256,12,256]{2,1,0:T(8,128)(2,1)} async-done(((bf16[1,12,256]{2,1,0:T(8,128)(2,1)}), bf16[256,12,256]{2,1,0:T(8,128)(2,1)}) %all-gather.6.cloned.1.call-update) | async-done | bytes 1572880 | tf_op jit(solution)/shard_map/all_gather | solution.py:35
  981.5 3.7 reshape.18
  985.2 3.5 convolution_multiply_fusion
  988.8 98.1 %all-gather.4.cloned.1.call-done = bf16[1536,3072]{1,0:T(8,128)(2,1)} async-done(((bf16[192,3072]{1,0:T(8,128)(2,1)}), bf16[1536,3072]{1,0:T(8,128)(2,1)}) %all-gather.4.cloned.1.call-update) | async-done | bytes 9437200 | tf_op jit(solution)/shard_map/all_gather | solution.py:12
  1086.9 9.2 convolution_convert_fusion
Async XLA Ops:
  7.2 2.0 copy-start
  7.2 275.0 %all-reduce.3.cloned.1.call-start = ((), (), s32[]{:S(2)}) async-start(), calls=%async_computation.2 | async-start | bytes 6291456
  15.4 966.1 %all-gather.6.cloned.1.call-start = ((), (), s32[]{:S(2)}) async-start(), calls=%async_computation.1 | async-start | bytes 2105344 | tf_op jit(solution)/shard_map/all_gather | solution.py:35
  286.3 800.6 %all-gather.4.cloned.1.call-start = ((), (), s32[]{:S(2)}) async-start(), calls=%async_computation | async-start | bytes 10616832 | tf_op jit(solution)/shard_map/all_gather | solution.py:12
Sparse Core Ops, SparseCore 0:
  15.5 266.6 all-reduce.2
  286.4 695.0 all-gather.5
  983.5 103.3 all-gather.3
where the time goes:
time: 1100 us
  waiting for transfers between devices  1060 us (96%)
  matrix products  18.9 us (2%)
  between operations  14.5 us (1%)
    all_gather x1, waiting for transfers between devices, on_device(): lax.all_gather(low_step, ('dp', 'fsdp'), axis=0, tiled=True)  695 us
    unnamed x4, waiting for transfers between devices  267 us
    all_gather x1, waiting for transfers between devices, on_device(): lax.all_gather(weight, 'fsdp', axis=0, tiled=True)  98.1 us
  transfers between devices with their start and end apart: 3, of which 3 were waited for; matrix products, arithmetic and copies ran while one was open for 1% of the time, Pallas kernels for 0%

commit v1 on v0

v1 whole, which is shorter than its diff:
```python
import functools

import jax
import jax.numpy as jnp
from jax import lax
from jax.experimental import pallas as pl
from jax.experimental.pallas import tpu as pltpu
from jax.sharding import PartitionSpec as P

MESH = pl.DeviceIdType.MESH
F32 = jnp.float32
BF16 = jnp.bfloat16
NX = 4
NY = 4


def kernel(
    nz, unit,
    attn_hbm, cot_hbm, w_hbm, proj_hbm, m1_hbm, m2_hbm, step_ref,
    gi_hbm, ws_hbm, fm_hbm, sm_hbm,
    attn, cot, wfull, proj, reduced, pown, csend, crecv, xsend, xrecv, zsend, zrecv, yrecv,
    m1, m2, fm, sm, low, gi, ws,
    load_sem, cload_sem, out_sem,
    c_ss, c_rs, x_ss, x_rs, z_ss, z_rs, y_ss, y_rs, m_ss, m_rs,
    lz_ss, lz_rs, lx_ss, lx_rs, lc_ss, lc_rs,
    wy_ss, wy_rs, wy2_ss, wy2_rs, wx_ss, wx_rs, wc_ss, wc_rs,
):
    rows = 4 * unit
    zrows = 8 * rows
    dp, fs = lax.axis_index("dp"), lax.axis_index("fsdp")
    z, xh, c = dp // 4, (dp // 2) % 2, dp % 2
    xl, y = fs // NY, fs % NY
    x = xh * 2 + xl
    oc = 1 - c

    def device(z_, x_, c_, y_):
        return (z_ * 4 + (x_ // 2) * 2 + c_, (x_ % 2) * NY + y_)

    sibling = device(z, x, oc, y)
    xdev = [None] + [device(z, (x + k) % NX, c, y) for k in (1, 2, 3)]
    ydev = [None] + [device(z, x, c, (y + k) % NY) for k in (1, 2, 3)]
    zdev = [None] + [device((z + k) % nz, x, c, y) for k in range(1, nz)]

    def remote(src, dst, ss, rs, dev):
        return pltpu.make_async_remote_copy(
            src_ref=src, dst_ref=dst, send_sem=ss, recv_sem=rs, device_id=dev, device_id_type=MESH
        )

    sent = []

    def send(*args):
        copy = remote(*args)
        copy.start()
        sent.append(copy)

    load_proj = pltpu.make_async_copy(proj_hbm, proj, load_sem.at[0])
    load_attn = pltpu.make_async_copy(attn_hbm, attn, load_sem.at[1])
    load_proj.start()
    load_attn.start()

    def load_cot(i):
        cols = pl.ds(pl.multiple_of(i * zrows, 128), zrows)
        return pltpu.make_async_copy(cot_hbm.at[:, cols], cot.at[:, cols], cload_sem.at[i])

    for i in range(nz):
        load_cot(i).start()
    own = xl * NY + y
    load_w = pltpu.make_async_copy(w_hbm, wfull.at[own], load_sem.at[2])
    load_w.start()
    load_m1 = pltpu.make_async_copy(m1_hbm, m1.at[y], load_sem.at[3])
    load_m2 = pltpu.make_async_copy(m2_hbm, m2.at[y], load_sem.at[4])
    load_m1.start()
    load_m2.start()

    barrier = pltpu.get_barrier_semaphore()
    partners = [sibling] + xdev[1:] + ydev[1:] + zdev[1:]
    for dev in partners:
        pl.semaphore_signal(barrier, inc=1, device_id=dev, device_id_type=MESH)
    pl.semaphore_wait(barrier, len(partners))

    yp, ym, xp, xm = ydev[1], ydev[3], xdev[1], xdev[3]

    def shard(other, dy):
        return ((1 - xl) if other else xl) * NY + (y + dy) % NY

    send(w_hbm.at[c], wfull.at[own, c], wy_ss.at[0], wy_rs.at[0], yp)
    send(w_hbm.at[c], wfull.at[own, c], wy_ss.at[1], wy_rs.at[1], ym)

    def weight_x(dy, src0, src1):
        s = shard(False, dy)
        send(src0, wfull.at[s, c, 0], wx_ss.at[dy, 0], wx_rs.at[dy, 0], xp)
        send(src1, wfull.at[s, c, 1], wx_ss.at[dy, 1], wx_rs.at[dy, 1], xm)

    def weight_core(other, dy):
        s = shard(other, dy)
        part = wfull.at[s, c]
        send(part, part, wc_ss.at[other, dy], wc_rs.at[other, dy], sibling)

    def weight_core_wait(other, dy):
        part = wfull.at[shard(other, dy), oc]
        remote(part, part, wc_ss.at[other, dy], wc_rs.at[other, dy], sibling).wait_recv()

    weight_x(0, w_hbm.at[c, 0], w_hbm.at[c, 1])

    for k in (1, 2, 3):
        send(m1_hbm, m1.at[y], m_ss.at[0, k - 1], m_rs.at[0, k - 1], ydev[k])
        send(m2_hbm, m2.at[y], m_ss.at[1, k - 1], m_rs.at[1, k - 1], ydev[k])

    load_proj.wait()
    load_attn.wait()
    reduced[...] = jnp.dot(attn[...], proj[...], preferred_element_type=F32).astype(BF16)

    def core_copy(i):
        return remote(csend.at[i], crecv.at[i], c_ss.at[i], c_rs.at[i], sibling)

    def part_step(i, carry):
        load_cot(i).wait()
        cols = pl.ds(pl.multiple_of(i * zrows, 128), zrows)
        part = lax.dot_general(
            cot[:, cols], reduced[...], (((0,), (0,)), ((), ())), preferred_element_type=F32
        ).reshape(2, 2, 2 * rows, -1)
        mine = c == 0
        pown[i] = jnp.where(mine, part[:, 0], part[:, 1])
        csend[i] = jnp.where(mine, part[:, 1], part[:, 0]).astype(BF16)
        core_copy(i).start()
        return carry

    lax.fori_loop(0, nz, part_step, 0)

    half = nz // 2

    def x_sum(i, carry):
        core_copy(i).wait_recv()
        total = (pown[i] + crecv[i].astype(F32)).astype(BF16).reshape(4, rows, -1)
        for k in range(4):
            xsend[k, i] = total[k]
        return carry

    for h in range(2):
        lax.fori_loop(h * half, (h + 1) * half, x_sum, 0)
        part = pl.ds(h * half, half)
        for k in (1, 3, 2):
            send(
                xsend.at[(x + k) % NX, part], xrecv.at[x, part],
                x_ss.at[h, k - 1], x_rs.at[h, k - 1], xdev[k],
            )

    def from_y(k):
        s = wfull.at[shard(False, k), c]
        remote(s, s, wy_ss.at[0], wy_rs.at[0 if k == 3 else 1], ydev[k]).wait_recv()

    from_y(3)
    part = wfull.at[shard(False, 3), c, 0]
    send(part, part, wy2_ss.at[0], wy2_rs.at[0], yp)
    from_y(1)
    part = wfull.at[shard(False, 1), c, 1]
    send(part, part, wy2_ss.at[1], wy2_rs.at[1], ym)
    for dy in (3, 1):
        s = shard(False, dy)
        weight_x(dy, wfull.at[s, c, 0], wfull.at[s, c, 1])
        weight_core(0, dy)

    for h in range(2):
        part = pl.ds(h * half, half)
        for k in (1, 2, 3):
            slot = xrecv.at[(x + k) % NX, part]
            remote(slot, slot, x_ss.at[h, 0], x_rs.at[h, 3 - k], xdev[k]).wait_recv()

    def z_sum(i, carry):
        total = xsend[x, i].astype(F32)
        for k in (1, 2, 3):
            total += xrecv[(x + k) % NX, i].astype(F32)
        zsend[i] = total.astype(BF16)
        return carry

    lax.fori_loop(0, nz, z_sum, 0)
    for k in range(1, nz):
        send(zsend.at[(z + k) % nz], zrecv.at[z], z_ss.at[k - 1], z_rs.at[k - 1], zdev[k])

    s2 = shard(False, 2)
    part = wfull.at[s2, c, 0]
    remote(part, part, wy2_ss.at[0], wy2_rs.at[0], ym).wait_recv()
    part = wfull.at[s2, c, 1]
    remote(part, part, wy2_ss.at[1], wy2_rs.at[1], yp).wait_recv()
    weight_x(2, wfull.at[s2, c, 0], wfull.at[s2, c, 1])
    weight_core(0, 2)

    for k in range(1, nz):
        slot = zrecv.at[(z + k) % nz]
        remote(slot, slot, z_ss.at[0], z_rs.at[nz - 1 - k], zdev[k]).wait_recv()
    total = zsend[z].astype(F32)
    for k in range(1, nz):
        total += zrecv[(z + k) % nz].astype(F32)
    yrecv[y] = total.astype(BF16)
    for k in (1, 2, 3):
        send(yrecv.at[y], yrecv.at[y], y_ss.at[k - 1], y_rs.at[k - 1], ydev[k])

    load_w.wait()
    load_m1.wait()
    load_m2.wait()

    grad_copies = []

    def grad(other, pair):
        q = ((1 - xl) if other else xl) * 2 + pair
        w = wfull[pl.ds(2 * q, 2)].reshape(-1, wfull.shape[-1])
        width = w.shape[0]
        gi[q] = lax.dot_general(
            cot[...], w, (((1,), (1,)), ((), ())), preferred_element_type=F32
        ).astype(BF16)
        cols = pl.ds(pl.multiple_of(q * width, 128), width)
        copy = pltpu.make_async_copy(gi.at[q], gi_hbm.at[:, cols], out_sem.at[2 * other + pair])
        copy.start()
        grad_copies.append(copy)

    for dy in (1, 2, 3):
        weight_core_wait(0, dy)
    grad(0, 0)

    for k in (1, 2, 3):
        slot = yrecv.at[(y + k) % NY]
        remote(slot, slot, y_ss.at[0], y_rs.at[3 - k], ydev[k]).wait_recv()
        for j, m in enumerate((m1, m2)):
            slot = m.at[(y + k) % NY]
            remote(slot, slot, m_ss.at[j, 0], m_rs.at[j, 3 - k], ydev[k]).wait_recv()
    projected = (
        yrecv[0].astype(F32) + yrecv[1].astype(F32) + yrecv[2].astype(F32) + yrecv[3].astype(F32)
    )
    projected = projected.reshape(NY, unit, -1)
    first = 0.9 * m1[...] + 0.1 * projected
    second = 0.999 * m2[...] + 0.001 * projected * projected
    fm[...] = first
    sm[...] = second
    steps = jnp.full((1, first.shape[-1]), step_ref[0], jnp.int32).astype(F32)
    first_hat = first / (1.0 - jnp.power(F32(0.9), steps))
    second_hat = second / (1.0 - jnp.power(F32(0.999), steps))
    low_step = first_hat / (jnp.sqrt(second_hat) + 1e-08)
    low[z, xh, c, xl] = low_step.reshape(rows, -1).astype(BF16)
    mine = low.at[z, xh, c, xl]
    for k in range(1, nz):
        send(mine, mine, lz_ss.at[k - 1], lz_rs.at[k - 1], zdev[k])
    store_fm = pltpu.make_async_copy(fm.at[y], fm_hbm, load_sem.at[3])
    store_sm = pltpu.make_async_copy(sm.at[y], sm_hbm, load_sem.at[4])
    store_fm.start()
    store_sm.start()

    for dy in (0, 3, 1, 2):
        s = shard(True, dy)
        for q, dev in ((0, xm), (1, xp)):
            part = wfull.at[s, c, q]
            remote(part, part, wx_ss.at[dy, q], wx_rs.at[dy, q], dev).wait_recv()
        weight_core(1, dy)

    for k in range(1, nz):
        slot = low.at[(z + k) % nz, xh, c, xl]
        remote(slot, slot, lz_ss.at[0], lz_rs.at[nz - 1 - k], zdev[k]).wait_recv()
    mine = low.at[:, xh, c, xl]
    for k in (1, 3, 2):
        send(mine, mine, lx_ss.at[k - 1], lx_rs.at[k - 1], xdev[k])
    send(mine, mine, lc_ss.at[0], lc_rs.at[0], sibling)

    grad(0, 1)

    for k in (1, 2, 3):
        x_ = (x + k) % NX
        slot = low.at[:, x_ // 2, c, x_ % 2]
        remote(slot, slot, lx_ss.at[0], lx_rs.at[3 - k], xdev[k]).wait_recv()
        send(slot, slot, lc_ss.at[k], lc_rs.at[k], sibling)

    for dy in range(4):
        weight_core_wait(1, dy)
    grad(1, 0)

    for k in range(4):
        x_ = (x + k) % NX
        slot = low.at[:, x_ // 2, oc, x_ % 2]
        remote(slot, slot, lc_ss.at[k], lc_rs.at[k], sibling).wait_recv()

    span = ws.shape[0]
    mine_proj = proj[pl.ds(pl.multiple_of(fs * span, 64), span), :]

    def ws_copy(i):
        cols = pl.ds(pl.multiple_of(i * zrows, 128), zrows)
        return pltpu.make_async_copy(ws.at[:, cols], ws_hbm.at[:, cols], cload_sem.at[i])

    def ws_step(i, carry):
        cols = pl.ds(pl.multiple_of(i * zrows, 128), zrows)
        ws[:, cols] = 0.25 * lax.dot_general(
            mine_proj, low[i].reshape(zrows, -1), (((1,), (1,)), ((), ())),
            preferred_element_type=F32,
        )
        ws_copy(i).start()
        return carry

    lax.fori_loop(0, nz, ws_step, 0)
    grad(1, 1)

    for copy in sent:
        copy.wait_send()

    def finish(i, carry):
        core_copy(i).wait_send()
        ws_copy(i).wait()
        return carry

    lax.fori_loop(0, nz, finish, 0)
    for copy in grad_copies:
        copy.wait()
    store_fm.wait()
    store_sm.wait()


def on_device(nz, attn, cot, w, proj, m1, m2, steps):
    unit, rank = m1.shape
    tokens, inner = attn.shape
    width = cot.shape[1]
    rows = 4 * unit
    span = w.shape[0]
    q = span // 4
    dma = pltpu.SemaphoreType.DMA
    vm = pltpu.VMEM
    any_ = pl.BlockSpec(memory_space=pl.ANY)
    gi, ws, fm, sm = pl.pallas_call(
        functools.partial(kernel, nz, unit),
        out_shape=(
            jax.ShapeDtypeStruct((tokens, inner), BF16),
            jax.ShapeDtypeStruct((span, width), F32),
            jax.ShapeDtypeStruct(m1.shape, F32),
            jax.ShapeDtypeStruct(m2.shape, F32),
        ),
        in_specs=[any_] * 6 + [pl.BlockSpec(memory_space=pltpu.SMEM)],
        out_specs=(any_,) * 4,
        scratch_shapes=[
            vm((tokens, inner), BF16),
            vm((tokens, width), BF16),
            vm((8, 2, 2, q, width), BF16),
            vm((inner, rank), BF16),
            vm((tokens, rank), BF16),
            vm((nz, 2, 2 * rows, rank), F32),
            vm((nz, 2, 2 * rows, rank), BF16),
            vm((nz, 2, 2 * rows, rank), BF16),
            vm((4, nz, rows, rank), BF16),
            vm((4, nz, rows, rank), BF16),
            vm((nz, rows, rank), BF16),
            vm((nz, rows, rank), BF16),
            vm((4, rows, rank), BF16),
            vm((4, unit, rank), F32),
            vm((4, unit, rank), F32),
            vm((4, unit, rank), F32),
            vm((4, unit, rank), F32),
            vm((nz, 2, 2, 2, rows, rank), BF16),
            vm((4, tokens, 2 * span), BF16),
            vm((span, width), F32),
            dma((5,)), dma((nz,)), dma((4,)),
            dma((nz,)), dma((nz,)),
            dma((2, 3)), dma((2, 3)),
            dma((nz - 1,)), dma((nz - 1,)),
            dma((3,)), dma((3,)),
            dma((2, 3)), dma((2, 3)),
            dma((nz - 1,)), dma((nz - 1,)),
            dma((3,)), dma((3,)),
            dma((4,)), dma((4,)),
            dma((2,)), dma((2,)),
            dma((2,)), dma((2,)),
            dma((4, 2)), dma((4, 2)),
            dma((2, 4)), dma((2, 4)),
        ],
        compiler_params=pltpu.CompilerParams(
            collective_id=0, has_side_effects=True, vmem_limit_bytes=56 * 2**20
        ),
    )(attn, cot, w.reshape(2, 2, q, width), proj, m1, m2, steps)
    return gi, ws, fm, sm


def solution(mesh):
    placed = (
        P(("dp", "fsdp"), None),
        P(("dp", "fsdp"), None),
        P("fsdp", None),
        P(),
        P(("dp", "fsdp"), None),
        P(("dp", "fsdp"), None),
        P(),
    )
    return jax.shard_map(
        functools.partial(on_device, mesh.shape["dp"] // 4),
        mesh=mesh,
        in_specs=placed,
        out_specs=(
            P(("dp", "fsdp"), None),
            P("fsdp", None),
            P(("dp", "fsdp"), None),
            P(("dp", "fsdp"), None),
        ),
        check_vma=False,
    )
```

time: 1100 us -> 69.7 us (0.06)
  waiting for transfers between devices: 1060 us -> 0 us
  Pallas kernels: 0 us -> 62.7 us
  matrix products: 18.9 us -> 0 us
  between operations: 14.5 us -> 1.3 us
    all_gather x2 -> x0, waiting for transfers between devices: 793 us -> none  [the longest x1 695 us: on_device(): lax.all_gather(low_step, ('dp', 'fsdp'), axis=0, tiled=True)]
    unnamed x4 -> x0, waiting for transfers between devices: 267 us -> none
    pallas_call x0 -> x1, Pallas kernels: none -> 62.7 us  [on_device(): pl.pallas_call(functools.partial(kernel, nz, unit), out_shape=(jax.ShapeD...]
    dot_general x3 -> x0, matrix products: 18.9 us -> none  [the longest x1 9.15 us: on_device(): lax.dot_general(cotangent, lax.all_gather(weight, 'fsdp', axis=0, tiled=T...]
  transfers between devices with their start and end apart: 3 -> 0, of which waited for: 3 -> 0; matrix products, arithmetic and copies ran while one was open for 1% -> 0% of each run, Pallas kernels for 0% -> 0%
where the time goes in v1:
time: 69.7 us; the launch traced here: 69.6 us
  Pallas kernels  62.7 us (90%)
  local copies, waits for them, and re-layouts  5.57 us (8%)
  between operations  1.3 us (2%)
    pallas_call x1, Pallas kernels, on_device(): pl.pallas_call(functools.partial(kernel, nz, unit), out_shape=(jax.ShapeD...  62.7 us
    unnamed x10, local copies, waits for them, and re-layouts  5.57 us

profile of v1, /device:TPU:1, one launch (start us, length us, event | category | flops | bytes accessed | tf_op | source)
XLA Modules:
  0.0 69.6 jit_solution(733691765487386499)
XLA Ops:
  1.3 62.7 %shard_map.102 = (bf16[576,1536]{1,0:T(8,128)(2,1)}, f32[192,3072]{1,0:T(8,128)}, f32[12,256]{1,0:T(8,128)}, f32[12,256]{1,0:T(8,128)}) custom-call(bf16[576,1536]{1,0:T(8,128)(2,1)} %attn_hbm.1, bf16[576,3072]{1,0:T(8,128)(2,1)} %cot_hbm.1, bf16[2,2,48,3072]{3,2,1,0:T(8,128)(2,1)} %bitcast.1, bf16[1536,256]{1,0:T(8,128)(2,1)} %proj_hbm.1, ...), custom_call_target="tpu_custom_call" | custom-call | tf_op jit(solution)/shard_map/pallas_call | solution.py:323
  64.0 0.0 copy-start
  64.0 2.9 %copy.16 = bf16[576,1536]{1,0:T(8,128)(2,1)} copy(bf16[576,1536]{1,0:T(8,128)(2,1)} %get-tuple-element.8) | data formatting | bytes 3538944
  67.0 0.0 copy-done
  67.0 0.0 copy-start.2
  67.0 0.0 copy-start.1
  67.0 1.4 %copy.17 = f32[192,3072]{1,0:T(8,128)} copy(f32[192,3072]{1,0:T(8,128)S(1)} %copy-done) | data formatting | bytes 4718592
  68.4 0.0 copy-done.2
  68.4 0.6 copy.18
  69.0 0.0 copy-done.1
  69.0 0.6 copy.19
Async XLA Ops:
  64.0 3.0 %copy-start = (f32[192,3072]{1,0:T(8,128)S(1)}, f32[192,3072]{1,0:T(8,128)}, u32[]{:S(2)}) copy-start(f32[192,3072]{1,0:T(8,128)} %get-tuple-element.9) | copy-start | bytes 7077892
  67.0 1.4 %copy-start.2 = (f32[12,256]{1,0:T(8,128)S(1)}, f32[12,256]{1,0:T(8,128)}, u32[]{:S(2)}) copy-start(f32[12,256]{1,0:T(8,128)} %get-tuple-element.10) | copy-start | bytes 36868
  67.0 2.0 %copy-start.1 = (f32[12,256]{1,0:T(8,128)S(1)}, f32[12,256]{1,0:T(8,128)}, u32[]{:S(2)}) copy-start(f32[12,256]{1,0:T(8,128)} %get-tuple-element.11) | copy-start | bytes 36868

commit v2 on v1

--- a/solution.py
+++ b/solution.py
@@ -17,13 +17,13 @@
 def kernel(
     nz, unit,
     attn_hbm, cot_hbm, w_hbm, proj_hbm, m1_hbm, m2_hbm, step_ref,
-    gi_hbm, ws_hbm, fm_hbm, sm_hbm,
+    gi, low, proj_mine, fm_mine, sm_mine,
     attn, cot, wfull, proj, reduced, pown, csend, crecv, xsend, xrecv, zsend, zrecv, yrecv,
-    m1, m2, fm, sm, low, gi, ws,
-    load_sem, cload_sem, out_sem,
+    m1, m2, fm, sm,
+    load_sem, cload_sem,
     c_ss, c_rs, x_ss, x_rs, z_ss, z_rs, y_ss, y_rs, m_ss, m_rs,
-    lz_ss, lz_rs, lx_ss, lx_rs, lc_ss, lc_rs,
-    wy_ss, wy_rs, wy2_ss, wy2_rs, wx_ss, wx_rs, wc_ss, wc_rs,
+    lz_ss, lz_rs, lx_ss, lx_rs, ly_ss, ly_rs, lc_ss, lc_rs,
+    wy_ss, wy_rs, wy2_ss, wy2_rs, wx_ss, wx_rs, wz_ss, wz_rs, wc_ss, wc_rs, wo_ss, wo_rs,
 ):
     rows = 4 * unit
     zrows = 8 * rows
@@ -78,29 +78,57 @@
         pl.semaphore_signal(barrier, inc=1, device_id=dev, device_id_type=MESH)
     pl.semaphore_wait(barrier, len(partners))
 
-    yp, ym, xp, xm = ydev[1], ydev[3], xdev[1], xdev[3]
+    yp, ym, xp, xm, zp, zm = ydev[1], ydev[3], xdev[1], xdev[3], zdev[1], zdev[nz - 1]
+    rx = z % 2
+    rz = 1 - rx
+    hcol = w_hbm.shape[-1] // 2
+    colh = [pl.ds(0, hcol), pl.ds(hcol, hcol)]
 
     def shard(other, dy):
         return ((1 - xl) if other else xl) * NY + (y + dy) % NY
 
-    send(w_hbm.at[c], wfull.at[own, c], wy_ss.at[0], wy_rs.at[0], yp)
-    send(w_hbm.at[c], wfull.at[own, c], wy_ss.at[1], wy_rs.at[1], ym)
-
-    def weight_x(dy, src0, src1):
+    def weight_x(dy, from_hbm=False):
         s = shard(False, dy)
-        send(src0, wfull.at[s, c, 0], wx_ss.at[dy, 0], wx_rs.at[dy, 0], xp)
-        send(src1, wfull.at[s, c, 1], wx_ss.at[dy, 1], wx_rs.at[dy, 1], xm)
-
-    def weight_core(other, dy):
+        for j, dev in ((0, xp), (1, xm)):
+            src = w_hbm.at[c, rx, :, colh[j]] if from_hbm else wfull.at[s, c, rx, :, colh[j]]
+            send(src, wfull.at[s, c, rx, :, colh[j]], wx_ss.at[dy, j], wx_rs.at[dy, j], dev)
+
+    def weight_x_to_z(dy):
+        s = shard(True, dy)
+        for j, src, dst in ((0, xm, zp), (1, xp, zm)):
+            part = wfull.at[s, c, rx, :, colh[j]]
+            remote(part, part, wx_ss.at[dy, j], wx_rs.at[dy, j], src).wait_recv()
+            send(part, part, wz_ss.at[dy, j], wz_rs.at[dy, j], dst)
+        part = wfull.at[s, c, rx]
+        send(part, part, wo_ss.at[dy, 0], wo_rs.at[dy, 0], sibling)
+
+    def weight_z_to_core(dy):
+        s = shard(True, dy)
+        for j, src in ((0, zm), (1, zp)):
+            part = wfull.at[s, c, rz, :, colh[j]]
+            remote(part, part, wz_ss.at[dy, j], wz_rs.at[dy, j], src).wait_recv()
+        part = wfull.at[s, c, rz]
+        send(part, part, wo_ss.at[dy, 1], wo_rs.at[dy, 1], sibling)
+
+    def weight_core(dy):
+        part = wfull.at[shard(False, dy), c]
+        send(part, part, wc_ss.at[dy - 1], wc_rs.at[dy - 1], sibling)
+
+    def weight_core_wait(other, dy):
         s = shard(other, dy)
-        part = wfull.at[s, c]
-        send(part, part, wc_ss.at[other, dy], wc_rs.at[other, dy], sibling)
-
-    def weight_core_wait(other, dy):
-        part = wfull.at[shard(other, dy), oc]
-        remote(part, part, wc_ss.at[other, dy], wc_rs.at[other, dy], sibling).wait_recv()
-
-    weight_x(0, w_hbm.at[c, 0], w_hbm.at[c, 1])
+        if other:
+            for i, r in enumerate((rx, rz)):
+                part = wfull.at[s, oc, r]
+                remote(part, part, wo_ss.at[dy, i], wo_rs.at[dy, i], sibling).wait_recv()
+        else:
+            part = wfull.at[s, oc]
+            remote(part, part, wc_ss.at[dy - 1], wc_rs.at[dy - 1], sibling).wait_recv()
+
+    for i in range(2):
+        for d, dev in ((0, yp), (1, ym)):
+            r = i if d == 0 else 1 - i
+            send(w_hbm.at[c, r], wfull.at[own, c, r], wy_ss.at[d, r], wy_rs.at[d, r], dev)
+    weight_x(0, True)
 
     for k in (1, 2, 3):
         send(m1_hbm, m1.at[y], m_ss.at[0, k - 1], m_rs.at[0, k - 1], ydev[k])
@@ -145,20 +173,23 @@
                 x_ss.at[h, k - 1], x_rs.at[h, k - 1], xdev[k],
             )
 
-    def from_y(k):
-        s = wfull.at[shard(False, k), c]
-        remote(s, s, wy_ss.at[0], wy_rs.at[0 if k == 3 else 1], ydev[k]).wait_recv()
-
-    from_y(3)
-    part = wfull.at[shard(False, 3), c, 0]
+    def from_y(k, r):
+        part = wfull.at[shard(False, k), c, r]
+        d = 0 if k == 3 else 1
+        remote(part, part, wy_ss.at[d, r], wy_rs.at[d, r], ydev[k]).wait_recv()
+        return part
+
+    part = from_y(3, 0)
     send(part, part, wy2_ss.at[0], wy2_rs.at[0], yp)
-    from_y(1)
-    part = wfull.at[shard(False, 1), c, 1]
+    part = from_y(1, 1)
     send(part, part, wy2_ss.at[1], wy2_rs.at[1], ym)
-    for dy in (3, 1):
-        s = shard(False, dy)
-        weight_x(dy, wfull.at[s, c, 0], wfull.at[s, c, 1])
-        weight_core(0, dy)
+    weight_x_to_z(0)
+    from_y(3, 1)
+    weight_x(3)
+    weight_core(3)
+    from_y(1, 0)
+    weight_x(1)
+    weight_core(1)
 
     for h in range(2):
         part = pl.ds(h * half, half)
@@ -178,12 +209,13 @@
         send(zsend.at[(z + k) % nz], zrecv.at[z], z_ss.at[k - 1], z_rs.at[k - 1], zdev[k])
 
     s2 = shard(False, 2)
-    part = wfull.at[s2, c, 0]
-    remote(part, part, wy2_ss.at[0], wy2_rs.at[0], ym).wait_recv()
-    part = wfull.at[s2, c, 1]
-    remote(part, part, wy2_ss.at[1], wy2_rs.at[1], yp).wait_recv()
-    weight_x(2, wfull.at[s2, c, 0], wfull.at[s2, c, 1])
-    weight_core(0, 2)
+    for r, dev in ((0, ym), (1, yp)):
+        part = wfull.at[s2, c, r]
+        remote(part, part, wy2_ss.at[r], wy2_rs.at[r], dev).wait_recv()
+    weight_x(2)
+    weight_core(2)
+    weight_x_to_z(3)
+    weight_x_to_z(1)
 
     for k in range(1, nz):
         slot = zrecv.at[(z + k) % nz]
@@ -199,19 +231,12 @@
     load_m1.wait()
     load_m2.wait()
 
-    grad_copies = []
-
     def grad(other, pair):
         q = ((1 - xl) if other else xl) * 2 + pair
         w = wfull[pl.ds(2 * q, 2)].reshape(-1, wfull.shape[-1])
-        width = w.shape[0]
         gi[q] = lax.dot_general(
             cot[...], w, (((1,), (1,)), ((), ())), preferred_element_type=F32
         ).astype(BF16)
-        cols = pl.ds(pl.multiple_of(q * width, 128), width)
-        copy = pltpu.make_async_copy(gi.at[q], gi_hbm.at[:, cols], out_sem.at[2 * other + pair])
-        copy.start()
-        grad_copies.append(copy)
 
     for dy in (1, 2, 3):
         weight_core_wait(0, dy)
@@ -235,79 +260,117 @@
     first_hat = first / (1.0 - jnp.power(F32(0.9), steps))
     second_hat = second / (1.0 - jnp.power(F32(0.999), steps))
     low_step = first_hat / (jnp.sqrt(second_hat) + 1e-08)
-    low[z, xh, c, xl] = low_step.reshape(rows, -1).astype(BF16)
-    mine = low.at[z, xh, c, xl]
+    low_step = low_step.reshape(rows, -1).astype(BF16)
+    rank_half = low_step.shape[-1] // 2
+    jy = y % 2
+    low[jy, z, xh, c, xl] = jnp.where(jy == 0, low_step[:, :rank_half], low_step[:, rank_half:])
+    mine = low.at[jy, z, xh, c, xl]
     for k in range(1, nz):
         send(mine, mine, lz_ss.at[k - 1], lz_rs.at[k - 1], zdev[k])
-    store_fm = pltpu.make_async_copy(fm.at[y], fm_hbm, load_sem.at[3])
-    store_sm = pltpu.make_async_copy(sm.at[y], sm_hbm, load_sem.at[4])
-    store_fm.start()
-    store_sm.start()
-
-    for dy in (0, 3, 1, 2):
-        s = shard(True, dy)
-        for q, dev in ((0, xm), (1, xp)):
-            part = wfull.at[s, c, q]
-            remote(part, part, wx_ss.at[dy, q], wx_rs.at[dy, q], dev).wait_recv()
-        weight_core(1, dy)
+    fm_mine[...] = fm[y]
+    sm_mine[...] = sm[y]
+    span = proj_mine.shape[0]
+    proj_mine[...] = proj[pl.ds(pl.multiple_of(fs * span, 64), span), :]
+
+    weight_x_to_z(2)
+    for dy in (0, 3, 1):
+        weight_z_to_core(dy)
 
     for k in range(1, nz):
-        slot = low.at[(z + k) % nz, xh, c, xl]
+        slot = low.at[jy, (z + k) % nz, xh, c, xl]
         remote(slot, slot, lz_ss.at[0], lz_rs.at[nz - 1 - k], zdev[k]).wait_recv()
-    mine = low.at[:, xh, c, xl]
+
+    def low_part(j, k, c_):
+        x_ = (x + k) % NX
+        return low.at[j, :, x_ // 2, c_, x_ % 2]
+
+    def low_zhalf(j, k, h):
+        x_ = (x + k) % NX
+        return low.at[j, pl.ds(h * half, half), x_ // 2, c, x_ % 2]
+
+    def low_spread(k):
+        for h, dev in ((0, yp), (1, ym)):
+            part = low_zhalf(jy, k, h)
+            send(part, part, ly_ss.at[k, h], ly_rs.at[k, h], dev)
+        part = low_part(jy, k, c)
+        send(part, part, lc_ss.at[0, k], lc_rs.at[0, k], sibling)
+
+    mine = low_part(jy, 0, c)
     for k in (1, 3, 2):
         send(mine, mine, lx_ss.at[k - 1], lx_rs.at[k - 1], xdev[k])
-    send(mine, mine, lc_ss.at[0], lc_rs.at[0], sibling)
+    low_spread(0)
 
     grad(0, 1)
-
-    for k in (1, 2, 3):
-        x_ = (x + k) % NX
-        slot = low.at[:, x_ // 2, c, x_ % 2]
+    weight_z_to_core(2)
+
+    for k in (1, 3, 2):
+        slot = low_part(jy, k, c)
         remote(slot, slot, lx_ss.at[0], lx_rs.at[3 - k], xdev[k]).wait_recv()
-        send(slot, slot, lc_ss.at[k], lc_rs.at[k], sibling)
+        low_spread(k)
 
     for dy in range(4):
         weight_core_wait(1, dy)
     grad(1, 0)
 
+    for k in (0, 1, 3, 2):
+        for h, dev in ((0, ym), (1, yp)):
+            part = low_zhalf(1 - jy, k, h)
+            remote(part, part, ly_ss.at[k, h], ly_rs.at[k, h], dev).wait_recv()
+        part = low_part(1 - jy, k, c)
+        send(part, part, lc_ss.at[1, k], lc_rs.at[1, k], sibling)
+
+    grad(1, 1)
+
     for k in range(4):
-        x_ = (x + k) % NX
-        slot = low.at[:, x_ // 2, oc, x_ % 2]
-        remote(slot, slot, lc_ss.at[k], lc_rs.at[k], sibling).wait_recv()
-
-    span = ws.shape[0]
-    mine_proj = proj[pl.ds(pl.multiple_of(fs * span, 64), span), :]
+        for i, j in ((0, jy), (1, 1 - jy)):
+            slot = low_part(j, k, oc)
+            remote(slot, slot, lc_ss.at[i, k], lc_rs.at[i, k], sibling).wait_recv()
+
+    for copy in sent:
+        copy.wait_send()
+
+    def finish(i, carry):
+        core_copy(i).wait_send()
+        return carry
+
+    lax.fori_loop(0, nz, finish, 0)
+
+
+def finish_kernel(gi, low, proj, fm, sm, gi_hbm, ws_hbm, fm_hbm, sm_hbm, ws, gi_sem, ws_sem, m_sem):
+    nz = low.shape[1]
+    width = gi.shape[-1]
+    copies = [
+        pltpu.make_async_copy(gi.at[q], gi_hbm.at[:, pl.ds(q * width, width)], gi_sem.at[q])
+        for q in range(4)
+    ]
+    copies.append(pltpu.make_async_copy(fm, fm_hbm, m_sem.at[0]))
+    copies.append(pltpu.make_async_copy(sm, sm_hbm, m_sem.at[1]))
+    for copy in copies:
+        copy.start()
+    zrows = ws.shape[1] // nz
 
     def ws_copy(i):
         cols = pl.ds(pl.multiple_of(i * zrows, 128), zrows)
-        return pltpu.make_async_copy(ws.at[:, cols], ws_hbm.at[:, cols], cload_sem.at[i])
+        return pltpu.make_async_copy(ws.at[:, cols], ws_hbm.at[:, cols], ws_sem.at[i])
 
     def ws_step(i, carry):
         cols = pl.ds(pl.multiple_of(i * zrows, 128), zrows)
+        rows = jnp.concatenate([low[j, i].reshape(zrows, -1) for j in range(2)], axis=1)
         ws[:, cols] = 0.25 * lax.dot_general(
-            mine_proj, low[i].reshape(zrows, -1), (((1,), (1,)), ((), ())),
-            preferred_element_type=F32,
+            proj[...], rows, (((1,), (1,)), ((), ())), preferred_element_type=F32
         )
         ws_copy(i).start()
         return carry
 
     lax.fori_loop(0, nz, ws_step, 0)
-    grad(1, 1)
-
-    for copy in sent:
-        copy.wait_send()
-
-    def finish(i, carry):
-        core_copy(i).wait_send()
+
+    def ws_wait(i, carry):
         ws_copy(i).wait()
         return carry
 
-    lax.fori_loop(0, nz, finish, 0)
-    for copy in grad_copies:
+    lax.fori_loop(0, nz, ws_wait, 0)
+    for copy in copies:
         copy.wait()
-    store_fm.wait()
-    store_sm.wait()
 
 
 def on_device(nz, attn, cot, w, proj, m1, m2, steps):
@@ -320,16 +383,17 @@
     dma = pltpu.SemaphoreType.DMA
     vm = pltpu.VMEM
     any_ = pl.BlockSpec(memory_space=pl.ANY)
-    gi, ws, fm, sm = pl.pallas_call(
+    results = pl.pallas_call(
         functools.partial(kernel, nz, unit),
         out_shape=(
-            jax.ShapeDtypeStruct((tokens, inner), BF16),
-            jax.ShapeDtypeStruct((span, width), F32),
-            jax.ShapeDtypeStruct(m1.shape, F32),
-            jax.ShapeDtypeStruct(m2.shape, F32),
+            vm((4, tokens, 2 * span), BF16),
+            vm((2, nz, 2, 2, 2, rows, rank // 2), BF16),
+            vm((span, rank), BF16),
+            vm(m1.shape, F32),
+            vm(m2.shape, F32),
         ),
-        in_specs=[any_] * 6 + [pl.BlockSpec(memory_space=pltpu.SMEM)],
-        out_specs=(any_,) * 4,
+        in_specs=[pl.BlockSpec(memory_space=pltpu.HBM)] * 6 + [pl.BlockSpec(memory_space=pltpu.SMEM)],
+        out_specs=(pl.BlockSpec(memory_space=vm),) * 5,
         scratch_shapes=[
             vm((tokens, inner), BF16),
             vm((tokens, width), BF16),
@@ -348,10 +412,7 @@
             vm((4, unit, rank), F32),
             vm((4, unit, rank), F32),
             vm((4, unit, rank), F32),
-            vm((nz, 2, 2, 2, rows, rank), BF16),
-            vm((4, tokens, 2 * span), BF16),
-            vm((span, width), F32),
-            dma((5,)), dma((nz,)), dma((4,)),
+            dma((5,)), dma((nz,)),
             dma((nz,)), dma((nz,)),
             dma((2, 3)), dma((2, 3)),
             dma((nz - 1,)), dma((nz - 1,)),
@@ -359,17 +420,38 @@
             dma((2, 3)), dma((2, 3)),
             dma((nz - 1,)), dma((nz - 1,)),
             dma((3,)), dma((3,)),
-            dma((4,)), dma((4,)),
-            dma((2,)), dma((2,)),
+            dma((4, 2)), dma((4, 2)),
+            dma((2, 4)), dma((2, 4)),
+            dma((2, 2)), dma((2, 2)),
             dma((2,)), dma((2,)),
             dma((4, 2)), dma((4, 2)),
-            dma((2, 4)), dma((2, 4)),
+            dma((4, 2)), dma((4, 2)),
+            dma((3,)), dma((3,)),
+            dma((4, 2)), dma((4, 2)),
         ],
         compiler_params=pltpu.CompilerParams(
-            collective_id=0, has_side_effects=True, vmem_limit_bytes=56 * 2**20
+            collective_id=0, has_side_effects=True, vmem_limit_bytes=40 * 2**20
         ),
-    )(attn, cot, w.reshape(2, 2, q, width), proj, m1, m2, steps)
-    return gi, ws, fm, sm
+    )(
+        *(
+            pltpu.with_memory_space_constraint(a, pltpu.HBM)
+            for a in (attn, cot, w.reshape(2, 2, q, width), proj, m1, m2)
+        ),
+        steps,
+    )
+    return pl.pallas_call(
+        finish_kernel,
+        out_shape=(
+            jax.ShapeDtypeStruct((tokens, inner), BF16),
+            jax.ShapeDtypeStruct((span, width), F32),
+            jax.ShapeDtypeStruct(m1.shape, F32),
+            jax.ShapeDtypeStruct(m2.shape, F32),
+        ),
+        in_specs=[pl.BlockSpec(memory_space=vm)] * 5,
+        out_specs=(any_,) * 4,
+        scratch_shapes=[vm((span, width), F32), dma((4,)), dma((nz,)), dma((2,))],
+        compiler_params=pltpu.CompilerParams(vmem_limit_bytes=16 * 2**20),
+    )(*(pltpu.with_memory_space_constraint(a, vm) for a in results))
 
 
 def solution(mesh):

time: 69.7 us -> 60.8 us (0.87)
  local copies, waits for them, and re-layouts: 5.57 us -> 0 us
  Pallas kernels: 62.7 us -> 59.4 us
    unnamed x10 -> x0, local copies, waits for them, and re-layouts: 5.57 us -> none
    pallas_call x1 -> x2, Pallas kernels: 62.7 us -> 59.4 us  [the longest x1 56.7 us: on_device(): pl.pallas_call(functools.partial(kernel, nz, unit), out_shape=(vm((4, tok...]
where the time goes in v2:
time: 60.8 us; the launch traced here: 60.7 us
  Pallas kernels  59.4 us (98%)
  between operations  1.29 us (2%)
    pallas_call x1, Pallas kernels, on_device(): pl.pallas_call(functools.partial(kernel, nz, unit), out_shape=(vm((4, tok...  56.7 us
    pallas_call x1, Pallas kernels, on_device(): pl.pallas_call(finish_kernel, out_shape=(jax.ShapeDtypeStruct((tokens, in...  2.74 us

profile of v2, /device:TPU:1, one launch (start us, length us, event | category | flops | bytes accessed | tf_op | source)
XLA Modules:
  0.0 60.7 jit_solution(9581534313843053261)
XLA Ops:
  1.3 56.7 %shard_map.102 = (bf16[4,576,384]{2,1,0:T(8,128)(2,1)S(1)}, bf16[2,8,2,2,2,48,128]{6,5,4,3,2,1,0:T(8,128)(2,1)S(1)}, bf16[192,256]{1,0:T(8,128)(2,1)S(1)}, f32[12,256]{1,0:T(8,128)S(1)}, f32[12,256]{1,0:T(8,128)S(1)}) custom-call(bf16[576,1536]{1,0:T(8,128)(2,1)} %attn_hbm.1, bf16[576,3072]{1,0:T(8,128)(2,1)} %cot_hbm.1, bf16[2,2,48,3072]{3,2,1,0:T(8,128)(2,1)} %bitcast.1, ...), custom_call_target="tpu_custom_call" | custom-call | tf_op jit(solution)/shard_map/pallas_call | solution.py:386
  57.9 2.7 %shard_map.103 = (bf16[576,1536]{1,0:T(8,128)(2,1)}, f32[192,3072]{1,0:T(8,128)}, f32[12,256]{1,0:T(8,128)}, f32[12,256]{1,0:T(8,128)}) custom-call(bf16[4,576,384]{2,1,0:T(8,128)(2,1)S(1)} %get-tuple-element.9.gi, bf16[2,8,2,2,2,48,128]{6,5,4,3,2,1,0:T(8,128)(2,1)S(1)} %get-tuple-element.10.low, bf16[192,256]{1,0:T(8,128)(2,1)S(1)} %get-tuple-element.11.proj, ...), custom_call_target="tpu_custom_call" | custom-call | tf_op jit(solution)/shard_map/pallas_call | solution.py:442

commit v3 on v0

v3 whole, which is shorter than its diff:
```python
import functools

import jax
import jax.numpy as jnp
from jax import lax
from jax.experimental import pallas as pl
from jax.experimental.pallas import tpu as pltpu
from jax.sharding import PartitionSpec as P

MESH = pl.DeviceIdType.MESH
F32 = jnp.float32
BF16 = jnp.bfloat16
NX = 4
NY = 4


def kernel(
    nz, unit,
    attn_hbm, cot_hbm, w_hbm, proj_hbm, m1_hbm, m2_hbm, step_ref,
    gi, low, proj_mine, fm_mine, sm_mine,
    attn, cot, wfull, proj, reduced, pown, csend, crecv, fsend, frecv, gsend, grecv, zsend, zrecv,
    m1, m2, fm, sm,
    load_sem, cload_sem,
    c_ss, c_rs, f_ss, f_rs, g_ss, g_rs, z_ss, z_rs, m_ss, m_rs, o_ss, o_rs,
    lz_ss, lz_rs, lg_ss, lg_rs, lf_ss, lf_rs, lc_ss, lc_rs,
    wy_ss, wy_rs, wy2_ss, wy2_rs, wx_ss, wx_rs, wz_ss, wz_rs, wc_ss, wc_rs,
):
    rows = 4 * unit
    zrows = 8 * rows
    ne = nz // NY
    dp, fs = lax.axis_index("dp"), lax.axis_index("fsdp")
    z, xh, c = dp // 4, (dp // 2) % 2, dp % 2
    xl, y = fs // NY, fs % NY
    x = xh * 2 + xl
    oc = 1 - c
    fme = x * oc + y * c
    gme = y * oc + x * c
    owner = z // ne
    owns = y == owner

    def device(z_, x_, c_, y_):
        return (z_ * 4 + (x_ // 2) * 2 + c_, (x_ % 2) * NY + y_)

    sibling = device(z, x, oc, y)
    xdev = [None] + [device(z, (x + k) % NX, c, y) for k in (1, 2, 3)]
    ydev = [None] + [device(z, x, c, (y + k) % NY) for k in (1, 2, 3)]
    zdev = [None] + [device((z + k) % nz, x, c, y) for k in range(1, nz)]
    fdev = [None] + [device(z, (x + k * oc) % NX, c, (y + k * c) % NY) for k in (1, 2, 3)]
    gdev = [None] + [device(z, (x + k * c) % NX, c, (y + k * oc) % NY) for k in (1, 2, 3)]
    owner_dev = device(z, x, c, owner)

    def remote(src, dst, ss, rs, dev):
        return pltpu.make_async_remote_copy(
            src_ref=src, dst_ref=dst, send_sem=ss, recv_sem=rs, device_id=dev, device_id_type=MESH
        )

    def send(*args):
        remote(*args).start()

    def arrive(part, rs):
        remote(part, part, rs, rs, sibling).wait_recv()

    def left(part, ss):
        remote(part, part, ss, ss, sibling).wait_send()

    load_proj = pltpu.make_async_copy(proj_hbm, proj, load_sem.at[0])
    load_attn = pltpu.make_async_copy(attn_hbm, attn, load_sem.at[1])
    load_proj.start()
    load_attn.start()

    def load_cot(i):
        cols = pl.ds(pl.multiple_of(i * zrows, 128), zrows)
        return pltpu.make_async_copy(cot_hbm.at[:, cols], cot.at[:, cols], cload_sem.at[i])

    load_cot(0).start()
    load_cot(1).start()
    own = xl * NY + y
    load_w = pltpu.make_async_copy(w_hbm, wfull.at[own], load_sem.at[2])
    load_m1 = pltpu.make_async_copy(m1_hbm, m1.at[y], load_sem.at[3])
    load_m2 = pltpu.make_async_copy(m2_hbm, m2.at[y], load_sem.at[4])

    barrier = pltpu.get_barrier_semaphore()
    partners = [sibling] + xdev[1:] + ydev[1:] + zdev[1:]
    for dev in partners:
        pl.semaphore_signal(barrier, inc=1, device_id=dev, device_id_type=MESH)
    pl.semaphore_wait(barrier, len(partners))

    yp, ym, xp, xm, zp, zm = ydev[1], ydev[3], xdev[1], xdev[3], zdev[1], zdev[nz - 1]
    rx = z % 2
    rz = 1 - rx
    hcol = w_hbm.shape[-1] // 2
    colh = [pl.ds(0, hcol), pl.ds(hcol, hcol)]

    def shard(other, dy):
        return ((1 - xl) if other else xl) * NY + (y + dy) % NY

    def half_rows(other, dy, r):
        return wfull.at[shard(other, dy), c, r]

    def piece(other, dy, r, j):
        return wfull.at[shard(other, dy), c, r, :, colh[j]]

    def weight_to_core(other, dy, i):
        part = half_rows(other, dy, (rx, rz)[i])
        n = other * 4 + dy
        send(part, part, wc_ss, wc_rs.at[n], sibling)

    def weight_from_core(other, dy):
        arrive(wfull.at[shard(other, dy), oc], wc_rs.at[other * 4 + dy])

    def weight_to_x(dy, from_hbm=False):
        for j, dev in ((0, xp), (1, xm)):
            part = piece(0, dy, rx, j)
            src = w_hbm.at[c, rx, :, colh[j]] if from_hbm else part
            send(src, part, wx_ss, wx_rs.at[dy], dev)

    def weight_from_x(dy):
        arrive(half_rows(1, dy, rx), wx_rs.at[dy])

    def weight_to_z(other, dy):
        for j in range(2):
            part = piece(other, dy, rx, j)
            send(part, part, wz_ss, wz_rs.at[other * 4 + dy], (zp, zm)[j])

    def weight_from_z(other, dy):
        arrive(half_rows(other, dy, rz), wz_rs.at[other * 4 + dy])
        weight_to_core(other, dy, 1)

    def weight_relay(i):
        for j, k, dev in ((0, 3, yp), (1, 1, ym)):
            part = piece(0, k, (rx, rz)[i], j)
            send(part, part, wy2_ss, wy2_rs.at[i], dev)

    def weight_from_relay(i):
        arrive(half_rows(0, 2, (rx, rz)[i]), wy2_rs.at[i])
        weight_to_core(0, 2, i)

    for d, dev in ((0, yp), (1, ym)):
        send(w_hbm.at[c, rx], half_rows(0, 0, rx), wy_ss, wy_rs.at[d], dev)
    weight_to_x(0, True)

    def moment_copy(j):
        src, dst = ((m1_hbm, m1), (m2_hbm, m2))[j]
        return remote(src, dst.at[y], m_ss.at[j], m_rs.at[j], owner_dev)

    @pl.when(jnp.logical_not(owns))
    def _():
        moment_copy(0).start()
        moment_copy(1).start()

    load_proj.wait()
    load_attn.wait()
    for i in range(2, nz):
        load_cot(i).start()
    reduced[...] = jnp.dot(attn[...], proj[...], preferred_element_type=F32).astype(BF16)

    def core_copy(i):
        return remote(csend.at[i], crecv.at[i], c_ss, c_rs.at[i], sibling)

    def part_step(i, carry):
        load_cot(i).wait()
        cols = pl.ds(pl.multiple_of(i * zrows, 128), zrows)
        part = lax.dot_general(
            cot[:, cols], reduced[...], (((0,), (0,)), ((), ())), preferred_element_type=F32
        ).reshape(2, 2, 2 * rows, -1)
        mine = c == 0
        pown[i] = jnp.where(mine, part[:, 0], part[:, 1])
        csend[i] = jnp.where(mine, part[:, 1], part[:, 0]).astype(BF16)
        core_copy(i).start()
        return carry

    lax.fori_loop(0, nz, part_step, 0)

    for load in (load_w, load_m1, load_m2):
        load.start()

    def core_sum(i, carry):
        core_copy(i).wait_recv()
        total = (pown[i] + crecv[i].astype(F32)).astype(BF16).reshape(4, rows, -1)
        q, e = i // ne, i % ne
        for x_ in range(NX):
            fsend[x_ * oc + q * c, q * oc + x_ * c, e] = total[x_]
        return carry

    lax.fori_loop(0, nz, core_sum, 0)
    for k in (1, 3, 2):
        send(fsend.at[(fme + k) % 4], frecv.at[fme], f_ss, f_rs, fdev[k])

    weight_from_x(0)
    weight_to_z(1, 0)
    weight_to_core(1, 0, 0)
    for d, k in ((0, 3), (1, 1)):
        arrive(half_rows(0, k, rx), wy_rs.at[d])
        weight_to_z(0, k)
    weight_relay(0)
    for k in (3, 1):
        weight_to_core(0, k, 0)

    arrive(frecv.at[pl.ds(0, 3)], f_rs)

    def f_sum(i, carry):
        total = fsend[fme, i].astype(F32)
        for k in (1, 2, 3):
            total += frecv[(fme + k) % 4, i].astype(F32)
        gsend[i] = total.astype(BF16)
        return carry

    lax.fori_loop(0, 4, f_sum, 0)
    for k in (1, 3, 2):
        send(gsend.at[(gme + k) % 4], grecv.at[gme], g_ss, g_rs, gdev[k])

    weight_to_x(3)
    weight_to_x(1)

    weight_from_relay(0)
    weight_to_x(2)

    arrive(grecv.at[pl.ds(0, 3)], g_rs)

    total = gsend[gme].astype(F32)
    for k in (1, 2, 3):
        total += grecv[(gme + k) % 4].astype(F32)
    zsend[...] = total.astype(BF16)

    def z_copy(e):
        z_ = ne * y + e
        return remote(zsend.at[e], zrecv.at[z], z_ss.at[e], z_rs, device(z_, x, c, y))

    for e in range(ne):
        @pl.when(ne * y + e != z)
        def _():
            z_copy(e).start()

    for k in (3, 1):
        weight_from_z(0, k)
    weight_relay(1)
    weight_from_z(1, 0)
    weight_from_x(3)
    weight_to_z(1, 3)
    weight_to_core(1, 3, 0)

    load_w.wait()
    load_m1.wait()
    load_m2.wait()

    mine = low.at[c, fme, gme, z % ne]

    def low_z_copy(k):
        return remote(mine, mine, lz_ss, lz_rs.at[z % ne], zdev[k])

    def moment_back(j, k):
        y_ = (y + k) % NY
        src, dst = ((fm, fm_mine), (sm, sm_mine))[j]
        return remote(src.at[y_], dst, o_ss.at[j], o_rs.at[j], ydev[k])

    @pl.when(owns)
    def _():
        arrive(zrecv.at[pl.ds(0, nz - 1)], z_rs)
        for j, m in enumerate((m1, m2)):
            arrive(m.at[pl.ds(0, 3)], m_rs.at[j])
        projected = zsend[z % ne].astype(F32)
        for k in range(1, nz):
            projected += zrecv[(z + k) % nz].astype(F32)
        projected = projected.reshape(NY, unit, -1)
        first = 0.9 * m1[...] + 0.1 * projected
        second = 0.999 * m2[...] + 0.001 * projected * projected
        steps = jnp.full((1, first.shape[-1]), step_ref[0], jnp.int32).astype(F32)
        first_hat = first / (1.0 - jnp.power(F32(0.9), steps))
        second_hat = second / (1.0 - jnp.power(F32(0.999), steps))
        low_step = first_hat / (jnp.sqrt(second_hat) + 1e-08)
        low[c, fme, gme, z % ne] = low_step.reshape(rows, -1).astype(BF16)
        for k in range(1, nz):
            low_z_copy(k).start()
        fm[...] = first
        sm[...] = second
        fm_mine[...] = fm[y]
        sm_mine[...] = sm[y]
        for j in range(2):
            for k in (1, 2, 3):
                moment_back(j, k).start()

    span = proj_mine.shape[0]
    proj_mine[...] = proj[pl.ds(pl.multiple_of(fs * span, 64), span), :]

    weight_from_x(1)
    weight_to_z(1, 1)
    weight_to_core(1, 1, 0)
    weight_from_relay(1)
    weight_from_x(2)
    weight_to_z(1, 2)
    weight_to_core(1, 2, 0)

    def grad(other, far):
        pair = y // 2
        q = ((1 - xl) if other else xl) * 2 + ((1 - pair) if far else pair)
        w = wfull[pl.ds(2 * q, 2)].reshape(-1, wfull.shape[-1])
        gi[q] = lax.dot_general(
            cot[...], w, (((1,), (1,)), ((), ())), preferred_element_type=F32
        ).astype(BF16)

    for dy in (3, 1):
        weight_from_core(0, dy)
    grad(0, 0)

    for e in range(ne):
        @pl.when(ne * y + e != z)
        def _():
            arrive(low.at[c, fme, gme, e], lz_rs.at[e])

    def low_to_f(k):
        part = low.at[c, fme, (gme + k) % 4]
        for i in (1, 3, 2):
            send(part, part, lf_ss, lf_rs.at[i - 1], fdev[i])

    def low_core(part):
        send(part, part, lc_ss, lc_rs, sibling)

    part = low.at[c, fme, gme]
    for k in (1, 3, 2):
        send(part, part, lg_ss, lg_rs.at[k - 1], gdev[k])
    low_to_f(0)

    weight_from_core(0, 2)
    grad(0, 1)

    for k in (1, 3, 2):
        arrive(low.at[c, fme, (gme + k) % 4], lg_rs.at[3 - k])
        low_to_f(k)
    low_core(low.at[c, fme])

    for dy in (3, 1, 2):
        weight_from_z(1, dy)

    for dy in (0, 3, 1):
        weight_from_core(1, dy)
    grad(1, 0)
    weight_from_core(1, 2)
    grad(1, 1)

    for k in (1, 3, 2):
        part = low.at[c, (fme + k) % 4]
        arrive(part, lf_rs.at[3 - k])
        low_core(part)

    arrive(low.at[oc], lc_rs)

    @pl.when(jnp.logical_not(owns))
    def _():
        arrive(fm_mine, o_rs.at[0])
        arrive(sm_mine, o_rs.at[1])
        moment_copy(0).wait_send()
        moment_copy(1).wait_send()

    @pl.when(owns)
    def _():
        left(zrecv.at[pl.ds(0, nz - 1)], lz_ss)
        for j, m in enumerate((fm, sm)):
            left(m.at[pl.ds(0, 3)], o_ss.at[j])

    for e in range(ne):
        @pl.when(ne * y + e != z)
        def _():
            z_copy(e).wait_send()

    left(csend, c_ss)
    left(fsend.at[pl.ds(0, 3)], f_ss)
    left(gsend.at[pl.ds(0, 3)], g_ss)
    left(low.at[c, fme, pl.ds(0, 3)], lg_ss)
    left(low.at[c, pl.ds(0, 3)], lf_ss)
    left(low.at[c], lc_ss)
    left(wfull.at[0, 0], wy_ss)
    left(wfull.at[0, 0], wy2_ss)
    left(wfull.at[0], wx_ss)
    left(wfull.at[pl.ds(0, 3), 0], wz_ss)
    left(wfull.at[pl.ds(0, 7), 0], wc_ss)


def finish_kernel(gi, low, proj, fm, sm, gi_hbm, ws_hbm, fm_hbm, sm_hbm, ws, gi_sem, ws_sem, m_sem):
    ne = low.shape[3]
    nz = NY * ne
    width = gi.shape[-1]
    copies = [
        pltpu.make_async_copy(gi.at[q], gi_hbm.at[:, pl.ds(q * width, width)], gi_sem.at[q])
        for q in range(4)
    ]
    copies.append(pltpu.make_async_copy(fm, fm_hbm, m_sem.at[0]))
    copies.append(pltpu.make_async_copy(sm, sm_hbm, m_sem.at[1]))
    for copy in copies:
        copy.start()
    zrows = ws.shape[1] // nz

    def ws_copy(i):
        cols = pl.ds(pl.multiple_of(i * zrows, 128), zrows)
        return pltpu.make_async_copy(ws.at[:, cols], ws_hbm.at[:, cols], ws_sem.at[i])

    def ws_step(i, carry):
        cols = pl.ds(pl.multiple_of(i * zrows, 128), zrows)
        q, e = i // ne, i % ne
        rows = []
        for xh in range(2):
            rows += [low[0, 2 * xh + xl, q, e] for xl in range(2)]
            rows += [low[1, q, 2 * xh + xl, e] for xl in range(2)]
        ws[:, cols] = 0.25 * lax.dot_general(
            proj[...], jnp.concatenate(rows, axis=0), (((1,), (1,)), ((), ())),
            preferred_element_type=F32,
        )
        ws_copy(i).start()
        return carry

    lax.fori_loop(0, nz, ws_step, 0)

    def ws_wait(i, carry):
        ws_copy(i).wait()
        return carry

    lax.fori_loop(0, nz, ws_wait, 0)
    for copy in copies:
        copy.wait()


def on_device(nz, attn, cot, w, proj, m1, m2, steps):
    unit, rank = m1.shape
    tokens, inner = attn.shape
    width = cot.shape[1]
    rows = 4 * unit
    ne = nz // NY
    span = w.shape[0]
    q = span // 4
    dma = pltpu.SemaphoreType.DMA
    one = pltpu.SemaphoreType.DMA
    vm = pltpu.VMEM
    any_ = pl.BlockSpec(memory_space=pl.ANY)
    results = pl.pallas_call(
        functools.partial(kernel, nz, unit),
        out_shape=(
            vm((4, tokens, 2 * span), BF16),
            vm((2, 4, 4, ne, rows, rank), BF16),
            vm((span, rank), BF16),
            vm(m1.shape, F32),
            vm(m2.shape, F32),
        ),
        in_specs=[pl.BlockSpec(memory_space=pltpu.HBM)] * 6 + [pl.BlockSpec(memory_space=pltpu.SMEM)],
        out_specs=(pl.BlockSpec(memory_space=vm),) * 5,
        scratch_shapes=[
            vm((tokens, inner), BF16),
            vm((tokens, width), BF16),
            vm((8, 2, 2, q, width), BF16),
            vm((inner, rank), BF16),
            vm((tokens, rank), BF16),
            vm((nz, 2, 2 * rows, rank), F32),
            vm((nz, 2, 2 * rows, rank), BF16),
            vm((nz, 2, 2 * rows, rank), BF16),
            vm((4, 4, ne, rows, rank), BF16),
            vm((4, 4, ne, rows, rank), BF16),
            vm((4, ne, rows, rank), BF16),
            vm((4, ne, rows, rank), BF16),
            vm((ne, rows, rank), BF16),
            vm((nz, rows, rank), BF16),
            vm((NY, unit, rank), F32),
            vm((NY, unit, rank), F32),
            vm((NY, unit, rank), F32),
            vm((NY, unit, rank), F32),
            dma((5,)), dma((nz,)),
            one, dma((nz,)),
            one, one,
            one, one,
            dma((ne,)), one,
            dma((2,)), dma((2,)),
            dma((2,)), dma((2,)),
            one, dma((ne,)),
            one, dma((3,)),
            one, dma((3,)),
            one, one,
            one, dma((2,)),
            one, dma((2,)),
            one, dma((4,)),
            one, dma((8,)),
            one, dma((8,)),
        ],
        compiler_params=pltpu.CompilerParams(
            collective_id=0, has_side_effects=True, vmem_limit_bytes=40 * 2**20
        ),
    )(
        *(
            pltpu.with_memory_space_constraint(a, pltpu.HBM)
            for a in (attn, cot, w.reshape(2, 2, q, width), proj, m1, m2)
        ),
        steps,
    )
    return pl.pallas_call(
        finish_kernel,
        out_shape=(
            jax.ShapeDtypeStruct((tokens, inner), BF16),
            jax.ShapeDtypeStruct((span, width), F32),
            jax.ShapeDtypeStruct(m1.shape, F32),
            jax.ShapeDtypeStruct(m2.shape, F32),
        ),
        in_specs=[pl.BlockSpec(memory_space=vm)] * 5,
        out_specs=(any_,) * 4,
        scratch_shapes=[vm((span, width), F32), dma((4,)), dma((nz,)), dma((2,))],
        compiler_params=pltpu.CompilerParams(vmem_limit_bytes=16 * 2**20),
    )(*(pltpu.with_memory_space_constraint(a, vm) for a in results))


def solution(mesh):
    placed = (
        P(("dp", "fsdp"), None),
        P(("dp", "fsdp"), None),
        P("fsdp", None),
        P(),
        P(("dp", "fsdp"), None),
        P(("dp", "fsdp"), None),
        P(),
    )
    return jax.shard_map(
        functools.partial(on_device, mesh.shape["dp"] // 4),
        mesh=mesh,
        in_specs=placed,
        out_specs=(
            P(("dp", "fsdp"), None),
            P("fsdp", None),
            P(("dp", "fsdp"), None),
            P(("dp", "fsdp"), None),
        ),
        check_vma=False,
    )
```

time: 1100 us -> 57.9 us (0.05)
  waiting for transfers between devices: 1060 us -> 0 us
  Pallas kernels: 0 us -> 56.6 us
  matrix products: 18.9 us -> 0 us
  between operations: 14.5 us -> 1.29 us
    all_gather x2 -> x0, waiting for transfers between devices: 793 us -> none  [the longest x1 695 us: on_device(): lax.all_gather(low_step, ('dp', 'fsdp'), axis=0, tiled=True)]
    unnamed x4 -> x0, waiting for transfers between devices: 267 us -> none
    pallas_call x0 -> x2, Pallas kernels: none -> 56.6 us  [the longest x1 53.8 us: on_device(): pl.pallas_call(functools.partial(kernel, nz, unit), out_shape=(vm((4, tok...]
    dot_general x3 -> x0, matrix products: 18.9 us -> none  [the longest x1 9.15 us: on_device(): lax.dot_general(cotangent, lax.all_gather(weight, 'fsdp', axis=0, tiled=T...]
  transfers between devices with their start and end apart: 3 -> 0, of which waited for: 3 -> 0; matrix products, arithmetic and copies ran while one was open for 1% -> 0% of each run, Pallas kernels for 0% -> 0%
where the time goes in v3:
time: 57.9 us
  Pallas kernels  56.6 us (98%)
  between operations  1.29 us (2%)
    pallas_call x1, Pallas kernels, on_device(): pl.pallas_call(functools.partial(kernel, nz, unit), out_shape=(vm((4, tok...  53.8 us
    pallas_call x1, Pallas kernels, on_device(): pl.pallas_call(finish_kernel, out_shape=(jax.ShapeDtypeStruct((tokens, in...  2.79 us

profile of v3, /device:TPU:1, one launch (start us, length us, event | category | flops | bytes accessed | tf_op | source)
XLA Modules:
  0.0 57.9 jit_solution(6582299180355709439)
XLA Ops:
  1.3 53.8 %shard_map.102 = (bf16[4,576,384]{2,1,0:T(8,128)(2,1)S(1)}, bf16[2,4,4,2,48,256]{5,4,3,2,1,0:T(8,128)(2,1)S(1)}, bf16[192,256]{1,0:T(8,128)(2,1)S(1)}, f32[12,256]{1,0:T(8,128)S(1)}, f32[12,256]{1,0:T(8,128)S(1)}) custom-call(bf16[576,1536]{1,0:T(8,128)(2,1)} %attn_hbm.1, bf16[576,3072]{1,0:T(8,128)(2,1)} %cot_hbm.1, bf16[2,2,48,3072]{3,2,1,0:T(8,128)(2,1)} %bitcast.1, ...), custom_call_target="tpu_custom_call" | custom-call | tf_op jit(solution)/shard_map/pallas_call | solution.py:433
  55.1 2.8 %shard_map.103 = (bf16[576,1536]{1,0:T(8,128)(2,1)}, f32[192,3072]{1,0:T(8,128)}, f32[12,256]{1,0:T(8,128)}, f32[12,256]{1,0:T(8,128)}) custom-call(bf16[4,576,384]{2,1,0:T(8,128)(2,1)S(1)} %get-tuple-element.9.gi, bf16[2,4,4,2,48,256]{5,4,3,2,1,0:T(8,128)(2,1)S(1)} %get-tuple-element.10.low, bf16[192,256]{1,0:T(8,128)(2,1)S(1)} %get-tuple-element.11.proj, ...), custom_call_target="tpu_custom_call" | custom-call | tf_op jit(solution)/shard_map/pallas_call | solution.py:490

commit v4 on v3

--- a/solution.py
+++ b/solution.py
@@ -23,7 +23,7 @@
     load_sem, cload_sem,
     c_ss, c_rs, f_ss, f_rs, g_ss, g_rs, z_ss, z_rs, m_ss, m_rs, o_ss, o_rs,
     lz_ss, lz_rs, lg_ss, lg_rs, lf_ss, lf_rs, lc_ss, lc_rs,
-    wy_ss, wy_rs, wy2_ss, wy2_rs, wx_ss, wx_rs, wz_ss, wz_rs, wc_ss, wc_rs,
+    wy_ss, wy_rs, wy2_ss, wy2_rs, wf_ss, wf_rs, wx_ss, wx_rs, wz_ss, wz_rs, wc_ss, wc_rs,
 ):
     rows = 4 * unit
     zrows = 8 * rows
@@ -108,14 +108,26 @@
     def weight_from_core(other, dy):
         arrive(wfull.at[shard(other, dy), oc], wc_rs.at[other * 4 + dy])
 
-    def weight_to_x(dy, from_hbm=False):
+    def weight_to_x(dy, i, from_hbm=False):
+        r = (rx, rz)[i]
         for j, dev in ((0, xp), (1, xm)):
-            part = piece(0, dy, rx, j)
-            src = w_hbm.at[c, rx, :, colh[j]] if from_hbm else part
-            send(src, part, wx_ss, wx_rs.at[dy], dev)
-
-    def weight_from_x(dy):
-        arrive(half_rows(1, dy, rx), wx_rs.at[dy])
+            part = piece(0, dy, r, j)
+            src = w_hbm.at[c, r, :, colh[j]] if from_hbm else part
+            send(src, part, wx_ss, wx_rs.at[dy + 4 * i], dev)
+
+    def weight_from_x(dy, i):
+        arrive(half_rows(1, dy, (rx, rz)[i]), wx_rs.at[dy + 4 * i])
+        weight_to_core(1, dy, i)
+
+    def weight_far_to_y():
+        part = half_rows(1, 0, rz)
+        for d, dev in ((0, yp), (1, ym)):
+            send(part, part, wf_ss, wf_rs.at[d], dev)
+
+    def weight_far_from_y():
+        for d, k in ((0, 3), (1, 1)):
+            arrive(half_rows(1, k, rz), wf_rs.at[d])
+            weight_to_core(1, k, 1)
 
     def weight_to_z(other, dy):
         for j in range(2):
@@ -137,7 +149,7 @@
 
     for d, dev in ((0, yp), (1, ym)):
         send(w_hbm.at[c, rx], half_rows(0, 0, rx), wy_ss, wy_rs.at[d], dev)
-    weight_to_x(0, True)
+    weight_to_x(0, 0, True)
 
     def moment_copy(j):
         src, dst = ((m1_hbm, m1), (m2_hbm, m2))[j]
@@ -186,13 +198,11 @@
     for k in (1, 3, 2):
         send(fsend.at[(fme + k) % 4], frecv.at[fme], f_ss, f_rs, fdev[k])
 
-    weight_from_x(0)
+    weight_from_x(0, 0)
     weight_to_z(1, 0)
-    weight_to_core(1, 0, 0)
     for d, k in ((0, 3), (1, 1)):
         arrive(half_rows(0, k, rx), wy_rs.at[d])
         weight_to_z(0, k)
-    weight_relay(0)
     for k in (3, 1):
         weight_to_core(0, k, 0)
 
@@ -209,11 +219,10 @@
     for k in (1, 3, 2):
         send(gsend.at[(gme + k) % 4], grecv.at[gme], g_ss, g_rs, gdev[k])
 
-    weight_to_x(3)
-    weight_to_x(1)
-
-    weight_from_relay(0)
-    weight_to_x(2)
+    weight_relay(0)
+    weight_to_x(3, 0)
+    weight_from_z(1, 0)
+    weight_far_to_y()
 
     arrive(grecv.at[pl.ds(0, 3)], g_rs)
 
@@ -231,13 +240,13 @@
         def _():
             z_copy(e).start()
 
+    weight_to_x(1, 0)
+    weight_from_relay(0)
+    weight_to_x(2, 0)
+
     for k in (3, 1):
         weight_from_z(0, k)
     weight_relay(1)
-    weight_from_z(1, 0)
-    weight_from_x(3)
-    weight_to_z(1, 3)
-    weight_to_core(1, 3, 0)
 
     load_w.wait()
     load_m1.wait()
@@ -282,14 +291,6 @@
     span = proj_mine.shape[0]
     proj_mine[...] = proj[pl.ds(pl.multiple_of(fs * span, 64), span), :]
 
-    weight_from_x(1)
-    weight_to_z(1, 1)
-    weight_to_core(1, 1, 0)
-    weight_from_relay(1)
-    weight_from_x(2)
-    weight_to_z(1, 2)
-    weight_to_core(1, 2, 0)
-
     def grad(other, far):
         pair = y // 2
         q = ((1 - xl) if other else xl) * 2 + ((1 - pair) if far else pair)
@@ -302,6 +303,9 @@
         weight_from_core(0, dy)
     grad(0, 0)
 
+    for dy in (3, 1):
+        weight_from_x(dy, 0)
+
     for e in range(ne):
         @pl.when(ne * y + e != z)
         def _():
@@ -320,6 +324,11 @@
         send(part, part, lg_ss, lg_rs.at[k - 1], gdev[k])
     low_to_f(0)
 
+    weight_from_relay(1)
+    weight_to_x(2, 1)
+    weight_from_x(2, 0)
+    weight_far_from_y()
+
     weight_from_core(0, 2)
     grad(0, 1)
 
@@ -328,8 +337,7 @@
         low_to_f(k)
     low_core(low.at[c, fme])
 
-    for dy in (3, 1, 2):
-        weight_from_z(1, dy)
+    weight_from_x(2, 1)
 
     for dy in (0, 3, 1):
         weight_from_core(1, dy)
@@ -370,8 +378,9 @@
     left(low.at[c], lc_ss)
     left(wfull.at[0, 0], wy_ss)
     left(wfull.at[0, 0], wy2_ss)
-    left(wfull.at[0], wx_ss)
-    left(wfull.at[pl.ds(0, 3), 0], wz_ss)
+    left(wfull.at[0, 0], wf_ss)
+    left(wfull.at[pl.ds(0, 5), 0, 0], wx_ss)
+    left(wfull.at[pl.ds(0, 3), 0, 0], wz_ss)
     left(wfull.at[pl.ds(0, 7), 0], wc_ss)
 
 
@@ -390,30 +399,31 @@
     zrows = ws.shape[1] // nz
 
     def ws_copy(i):
-        cols = pl.ds(pl.multiple_of(i * zrows, 128), zrows)
+        cols = pl.ds(pl.multiple_of(i * 2 * zrows, 128), 2 * zrows)
         return pltpu.make_async_copy(ws.at[:, cols], ws_hbm.at[:, cols], ws_sem.at[i])
 
     def ws_step(i, carry):
-        cols = pl.ds(pl.multiple_of(i * zrows, 128), zrows)
-        q, e = i // ne, i % ne
-        rows = []
-        for xh in range(2):
-            rows += [low[0, 2 * xh + xl, q, e] for xl in range(2)]
-            rows += [low[1, q, 2 * xh + xl, e] for xl in range(2)]
-        ws[:, cols] = 0.25 * lax.dot_general(
-            proj[...], jnp.concatenate(rows, axis=0), (((1,), (1,)), ((), ())),
-            preferred_element_type=F32,
-        )
+        for n in range(2):
+            t = 2 * i + n
+            q, e = t // ne, t % ne
+            rows = []
+            for xh in range(2):
+                rows += [low[0, 2 * xh + xl, q, e] for xl in range(2)]
+                rows += [low[1, q, 2 * xh + xl, e] for xl in range(2)]
+            ws[:, pl.ds(pl.multiple_of(t * zrows, 128), zrows)] = 0.25 * lax.dot_general(
+                proj[...], jnp.concatenate(rows, axis=0), (((1,), (1,)), ((), ())),
+                preferred_element_type=F32,
+            )
         ws_copy(i).start()
         return carry
 
-    lax.fori_loop(0, nz, ws_step, 0)
+    lax.fori_loop(0, nz // 2, ws_step, 0)
 
     def ws_wait(i, carry):
         ws_copy(i).wait()
         return carry
 
-    lax.fori_loop(0, nz, ws_wait, 0)
+    lax.fori_loop(0, nz // 2, ws_wait, 0)
     for copy in copies:
         copy.wait()
 
@@ -473,7 +483,8 @@
             one, one,
             one, dma((2,)),
             one, dma((2,)),
-            one, dma((4,)),
+            one, dma((2,)),
+            one, dma((8,)),
             one, dma((8,)),
             one, dma((8,)),
         ],
@@ -497,7 +508,7 @@
         ),
         in_specs=[pl.BlockSpec(memory_space=vm)] * 5,
         out_specs=(any_,) * 4,
-        scratch_shapes=[vm((span, width), F32), dma((4,)), dma((nz,)), dma((2,))],
+        scratch_shapes=[vm((span, width), F32), dma((4,)), dma((nz // 2,)), dma((2,))],
         compiler_params=pltpu.CompilerParams(vmem_limit_bytes=16 * 2**20),
     )(*(pltpu.with_memory_space_constraint(a, vm) for a in results))
 

time: 57.9 us -> 55.6 us (0.960)
  Pallas kernels: 56.6 us -> 54.3 us
    pallas_call x1, Pallas kernels: 53.8 us -> 52.2 us  [on_device(): pl.pallas_call(functools.partial(kernel, nz, unit), out_shape=(vm((4, tok...]
    pallas_call x1, Pallas kernels: 2.79 us -> 2.1 us  [on_device(): pl.pallas_call(finish_kernel, out_shape=(jax.ShapeDtypeStruct((tokens, in...]
where the time goes in v4:
time: 55.6 us
  Pallas kernels  54.3 us (98%)
  between operations  1.29 us (2%)
    pallas_call x1, Pallas kernels, on_device(): pl.pallas_call(functools.partial(kernel, nz, unit), out_shape=(vm((4, tok...  52.2 us
    pallas_call x1, Pallas kernels, on_device(): pl.pallas_call(finish_kernel, out_shape=(jax.ShapeDtypeStruct((tokens, in...  2.1 us

profile of v4, /device:TPU:1, one launch (start us, length us, event | category | flops | bytes accessed | tf_op | source)
XLA Modules:
  0.0 55.6 jit_solution(10110162174234725436)
XLA Ops:
  1.3 52.2 %shard_map.102 = (bf16[4,576,384]{2,1,0:T(8,128)(2,1)S(1)}, bf16[2,4,4,2,48,256]{5,4,3,2,1,0:T(8,128)(2,1)S(1)}, bf16[192,256]{1,0:T(8,128)(2,1)S(1)}, f32[12,256]{1,0:T(8,128)S(1)}, f32[12,256]{1,0:T(8,128)S(1)}) custom-call(bf16[576,1536]{1,0:T(8,128)(2,1)} %attn_hbm.1, bf16[576,3072]{1,0:T(8,128)(2,1)} %cot_hbm.1, bf16[2,2,48,3072]{3,2,1,0:T(8,128)(2,1)} %bitcast.1, ...), custom_call_target="tpu_custom_call" | custom-call | tf_op jit(solution)/shard_map/pallas_call | solution.py:443
  53.5 2.1 %shard_map.103 = (bf16[576,1536]{1,0:T(8,128)(2,1)}, f32[192,3072]{1,0:T(8,128)}, f32[12,256]{1,0:T(8,128)}, f32[12,256]{1,0:T(8,128)}) custom-call(bf16[4,576,384]{2,1,0:T(8,128)(2,1)S(1)} %get-tuple-element.9.gi, bf16[2,4,4,2,48,256]{5,4,3,2,1,0:T(8,128)(2,1)S(1)} %get-tuple-element.10.low, bf16[192,256]{1,0:T(8,128)(2,1)S(1)} %get-tuple-element.11.proj, ...), custom_call_target="tpu_custom_call" | custom-call | tf_op jit(solution)/shard_map/pallas_call | solution.py:501

commit v5 on v4

--- a/solution.py
+++ b/solution.py
@@ -119,14 +119,15 @@
         arrive(half_rows(1, dy, (rx, rz)[i]), wx_rs.at[dy + 4 * i])
         weight_to_core(1, dy, i)
 
-    def weight_far_to_y():
-        part = half_rows(1, 0, rz)
-        for d, dev in ((0, yp), (1, ym)):
-            send(part, part, wf_ss, wf_rs.at[d], dev)
+    def weight_far_to_y(j):
+        part = piece(1, 0, rz, j)
+        for dev in (yp, ym):
+            send(part, part, wf_ss, wf_rs.at[j], dev)
 
     def weight_far_from_y():
-        for d, k in ((0, 3), (1, 1)):
-            arrive(half_rows(1, k, rz), wf_rs.at[d])
+        for j in range(2):
+            arrive(half_rows(1, 0, rz), wf_rs.at[j])
+        for k in (3, 1):
             weight_to_core(1, k, 1)
 
     def weight_to_z(other, dy):
@@ -222,7 +223,7 @@
     weight_relay(0)
     weight_to_x(3, 0)
     weight_from_z(1, 0)
-    weight_far_to_y()
+    weight_far_to_y(0)
 
     arrive(grecv.at[pl.ds(0, 3)], g_rs)
 
@@ -247,6 +248,7 @@
     for k in (3, 1):
         weight_from_z(0, k)
     weight_relay(1)
+    weight_far_to_y(1)
 
     load_w.wait()
     load_m1.wait()
@@ -303,6 +305,8 @@
         weight_from_core(0, dy)
     grad(0, 0)
 
+    weight_from_relay(1)
+    weight_to_x(2, 1)
     for dy in (3, 1):
         weight_from_x(dy, 0)
 
@@ -324,8 +328,6 @@
         send(part, part, lg_ss, lg_rs.at[k - 1], gdev[k])
     low_to_f(0)
 
-    weight_from_relay(1)
-    weight_to_x(2, 1)
     weight_from_x(2, 0)
     weight_far_from_y()
 

time: 55.6 us -> 55.4 us (level)
  no operation moved by 1% of the time
where the time goes in v5:
time: 55.4 us; the launch traced here: 55.3 us
  Pallas kernels  54 us (97%)
  between operations  1.29 us (2%)
    pallas_call x1, Pallas kernels, on_device(): pl.pallas_call(functools.partial(kernel, nz, unit), out_shape=(vm((4, tok...  51.9 us
    pallas_call x1, Pallas kernels, on_device(): pl.pallas_call(finish_kernel, out_shape=(jax.ShapeDtypeStruct((tokens, in...  2.09 us

profile of v5, /device:TPU:1, one launch (start us, length us, event | category | flops | bytes accessed | tf_op | source)
XLA Modules:
  0.0 55.3 jit_solution(14224783046211543261)
XLA Ops:
  1.3 51.9 %shard_map.102 = (bf16[4,576,384]{2,1,0:T(8,128)(2,1)S(1)}, bf16[2,4,4,2,48,256]{5,4,3,2,1,0:T(8,128)(2,1)S(1)}, bf16[192,256]{1,0:T(8,128)(2,1)S(1)}, f32[12,256]{1,0:T(8,128)S(1)}, f32[12,256]{1,0:T(8,128)S(1)}) custom-call(bf16[576,1536]{1,0:T(8,128)(2,1)} %attn_hbm.1, bf16[576,3072]{1,0:T(8,128)(2,1)} %cot_hbm.1, bf16[2,2,48,3072]{3,2,1,0:T(8,128)(2,1)} %bitcast.1, ...), custom_call_target="tpu_custom_call" | custom-call | tf_op jit(solution)/shard_map/pallas_call | solution.py:445
  53.2 2.1 %shard_map.103 = (bf16[576,1536]{1,0:T(8,128)(2,1)}, f32[192,3072]{1,0:T(8,128)}, f32[12,256]{1,0:T(8,128)}, f32[12,256]{1,0:T(8,128)}) custom-call(bf16[4,576,384]{2,1,0:T(8,128)(2,1)S(1)} %get-tuple-element.9.gi, bf16[2,4,4,2,48,256]{5,4,3,2,1,0:T(8,128)(2,1)S(1)} %get-tuple-element.10.low, bf16[192,256]{1,0:T(8,128)(2,1)S(1)} %get-tuple-element.11.proj, ...), custom_call_target="tpu_custom_call" | custom-call | tf_op jit(solution)/shard_map/pallas_call | solution.py:503
